TPU v7x, 256 devices: a whole 4x4x8 slice. The times are simulated.
256 devices in a mesh: dom: 32 (over y, x, core), head: 8 (over z).
Axes of the slice: x: 4, y: 4, z: 8, core: 2. Of those that a mesh axis runs over, the one named last changes fastest.
Arguments:
- embeds: bfloat16 [2, 1024, 3584], P(None, 'dom'), may hold values from -6 to 6
- ancestors: int32 [1024], replicated, may hold values from 0 to 1023, as said below
- lengths: int32 [1024], replicated, may hold values from 64 to 256
- kv_cache: bfloat16 [1024, 256, 8, 512], P('dom', None, 'head'), may hold values from -480 to 480, as said below
- attn_gain: float32 [3584], replicated, may hold values from 0.25 to 1.75
- w_query: bfloat16 [3584, 4096], P(None, 'head'), may hold values from -0.09375 to 0.09375
- w_keyval: bfloat16 [3584, 4096], P(None, 'head'), may hold values from -0.09375 to 0.09375
- w_out: bfloat16 [4096, 3584], P('head'), may hold values from -0.09375 to 0.09375
- post_gain: float32 [3584], replicated, may hold values from 0.25 to 1.75
- final_gain: float32 [3584], replicated, may hold values from 0.25 to 1.75
- twist_weight: float32 [3584], replicated, may hold values from -0.09375 to 0.09375
Outputs:
- hidden_out: bfloat16 [2, 1024, 3584], P(None, 'dom')
- twist: float32 [2, 1024], P(None, 'dom')
Inputs may be any that keep to these rules, and one draw needn't show every extreme that they name: The particles of one index of dom (an aligned block of 32 particles) have ancestors in exactly 16 distinct aligned blocks, exactly 2 particles in each, and all particles whose ancestors lie in one common aligned block have the same ancestor. `kv_cache`: cached keys and values are finite.
All inputs are finite; a program needn't handle non-finite values.
Results may differ from a plain program's by a relative error of at most 0.012.
The roundings to bfloat16 on the way count: a program that leaves them out, or rounds other values in their place, can miss the bound.
Values may be sent and summed in bfloat16 or wider, within the bound.
A program may use at most 128 MiB of HBM per device.

v0:
```python
import math

import jax
import jax.numpy as jnp
from jax import lax
from jax.sharding import PartitionSpec as P

EPSILON = 1e-06
SCORE_SCALE = 0.0625
MASKED_SCORE = -1e30
LOG_THETA = math.log(10000.0)


def normalize(values, gains):
    mean_square = jnp.mean(values * values, axis=-1, keepdims=True)
    return values * lax.rsqrt(mean_square + EPSILON) * gains


def rope_tables(positions, half_dim):
    inverse = jnp.exp(jnp.arange(half_dim, dtype=jnp.float32) * (-LOG_THETA / half_dim))
    angles = positions.astype(jnp.float32)[..., None] * inverse
    return (jnp.cos(angles), jnp.sin(angles))


def rotate(values, cosine, sine):
    half_dim = values.shape[-1] // 2
    first_half = values[..., :half_dim]
    second_half = values[..., half_dim:]
    return jnp.concatenate(
        [first_half * cosine - second_half * sine, second_half * cosine + first_half * sine],
        axis=-1,
    )


def prefix_partial(queries, kv_block, valid_len):
    head_dim = queries.shape[-1]
    cached_keys = kv_block[..., :head_dim]
    cached_values = kv_block[..., head_dim:]
    scores = (
        jnp.einsum("tgrh,cgh->tgrc", queries, cached_keys, preferred_element_type=jnp.float32)
        * SCORE_SCALE
    )
    valid = jnp.arange(kv_block.shape[0]) < valid_len
    scores = jnp.where(valid, scores, MASKED_SCORE)
    highest = jnp.max(scores, axis=-1)
    expo = jnp.exp(scores - highest[..., None])
    totals = jnp.sum(expo, axis=-1)
    weighted = jnp.einsum(
        "tgrc,cgh->tgrh",
        expo.astype(jnp.bfloat16),
        cached_values,
        preferred_element_type=jnp.float32,
    )
    return (highest, totals, weighted)


def fresh_partial(queries, new_keys, new_values):
    steps = queries.shape[0]
    scores = (
        jnp.einsum("tpgrh,upgh->tpgru", queries, new_keys, preferred_element_type=jnp.float32)
        * SCORE_SCALE
    )
    allowed = jnp.arange(steps)[None, :] <= jnp.arange(steps)[:, None]
    scores = jnp.where(allowed[:, None, None, None, :], scores, MASKED_SCORE)
    highest = jnp.max(scores, axis=-1)
    expo = jnp.exp(scores - highest[..., None])
    totals = jnp.sum(expo, axis=-1)
    weighted = jnp.einsum(
        "tpgru,upgh->tpgrh",
        expo.astype(jnp.bfloat16),
        new_values,
        preferred_element_type=jnp.float32,
    )
    return (highest, totals, weighted)


def merge_partials(cached, fresh):
    high_cached, total_cached, out_cached = cached
    high_fresh, total_fresh, out_fresh = fresh
    highest = jnp.maximum(high_cached, high_fresh)
    cached_factor = jnp.exp(high_cached - highest)
    fresh_factor = jnp.exp(high_fresh - highest)
    denominator = cached_factor * total_cached + fresh_factor * total_fresh
    return (
        cached_factor[..., None] * out_cached + fresh_factor[..., None] * out_fresh
    ) / denominator[..., None]


def per_device(
    embeds,
    ancestors,
    lengths,
    kv_cache,
    attn_gain,
    w_query,
    w_keyval,
    w_out,
    post_gain,
    final_gain,
    twist_weight,
):
    steps, local, width = embeds.shape
    heads = kv_cache.shape[2]
    head_dim = kv_cache.shape[3] // 2
    group = w_query.shape[1] // (heads * head_dim)
    peer_count = lax.axis_size("dom")
    my_index = lax.axis_index("dom")
    table = ancestors.reshape(peer_count, local)
    my_parents = lax.dynamic_index_in_dim(table, my_index, 0, keepdims=False)
    everyone = jnp.arange(ancestors.shape[0], dtype=jnp.int32)
    parent_len = jnp.sum(
        jnp.where(my_parents[:, None] == everyone[None, :], lengths[None, :], 0), axis=1
    )
    source_dev = my_parents // local
    hits = table // local == my_index
    chosen = jnp.maximum(jnp.max(jnp.where(hits, table % local, -1), axis=1), 0)
    served = jnp.take(kv_cache, chosen, axis=0)
    inputs = embeds.astype(jnp.float32)
    normed = normalize(inputs, attn_gain).astype(jnp.bfloat16).reshape(steps * local, width)
    queries = jnp.dot(normed, w_query, preferred_element_type=jnp.float32).reshape(
        steps, local, heads, group, head_dim
    )
    keyval = jnp.dot(normed, w_keyval, preferred_element_type=jnp.float32).reshape(
        steps, local, heads, 2, head_dim
    )
    positions = parent_len[None, :] + jnp.arange(steps, dtype=jnp.int32)[:, None]
    cosine, sine = rope_tables(positions, head_dim // 2)
    rotated = rotate(queries, cosine[:, :, None, None, :], sine[:, :, None, None, :]).astype(
        jnp.bfloat16
    )
    new_keys = rotate(keyval[:, :, :, 0, :], cosine[:, :, None, :], sine[:, :, None, :]).astype(
        jnp.bfloat16
    )
    new_values = keyval[:, :, :, 1, :].astype(jnp.bfloat16)
    received = lax.all_to_all(served, "dom", split_axis=0, concat_axis=0, tiled=True)
    blocks = jnp.take(received, source_dev, axis=0)
    cached = jax.vmap(prefix_partial, in_axes=(1, 0, 0), out_axes=1)(rotated, blocks, parent_len)
    fresh = fresh_partial(rotated, new_keys, new_values)
    attended = merge_partials(cached, fresh).astype(jnp.bfloat16)
    partial_proj = jnp.dot(
        attended.reshape(steps * local, -1), w_out, preferred_element_type=jnp.float32
    ).reshape(steps, local, width)
    projected = jnp.stack([lax.psum(partial_proj[step], "head") for step in range(steps)])
    updated = inputs + normalize(projected, post_gain)
    twist = jnp.sum(normalize(updated, final_gain) * twist_weight, axis=-1)
    return (updated.astype(jnp.bfloat16), twist)


def solution(mesh):
    in_specs = (
        P(None, "dom", None),
        P(),
        P(),
        P("dom", None, "head", None),
        P(),
        P(None, "head"),
        P(None, "head"),
        P("head", None),
        P(),
        P(),
        P(),
    )
    out_specs = (P(None, "dom", None), P(None, "dom"))
    return jax.shard_map(
        per_device, mesh=mesh, in_specs=in_specs, out_specs=out_specs, check_vma=False
    )
```

profile of v0, /device:TPU:24, one launch (start us, length us, event | category | flops | bytes accessed | tf_op | source)
XLA Modules:
  0.0 248.8 jit_solution(13032066481321791414)
XLA Ops:
  7.2 0.8 reshape.210
  7.9 0.1 fusion.48
  8.1 8.2 %gather_fusion = bf16[32,256,512]{2,1,0:T(8,128)(2,1)} fusion(bf16[32,256,512]{2,1,0:T(8,128)(2,1)} %bitcast.163, s32[1024]{0:T(1024)S(1)} %pad_clamp_fusion.1), kind=kCustom, calls=%fused_computation.clone | custom fusion | bytes 16777344 | tf_op jit(solution)/shard_map/jit(_take)/gather | solution.py:117
  16.3 7.5 %bitcast_select_fusion.1 = bf16[32,256,1,512]{3,1,2,0:T(8,128)(2,1)} fusion(bf16[32,256,512]{2,1,0:T(8,128)(2,1)} %gather_fusion, pred[32]{0:T(512)(128)(4,1)S(1)} %broadcast_compare_fusion), kind=kLoop, calls=%fused_computation.3 | loop fusion | flops 4194304 | bytes 16777248 | tf_op jit(solution)/shard_map/jit(_take)/select_n | solution.py:117
  23.7 7.3 %all-to-all-start = ((bf16[32,256,1,512]{3,1,2,0:T(8,128)(2,1)}), bf16[32,256,1,512]{3,1,2,0:T(8,128)(2,1)}, u32[]{:S(2)}, u32[]{:S(2)}) async-start(bf16[32,256,1,512]{3,1,2,0:T(8,128)(2,1)} %bitcast_select_fusion.1), calls=%async_computation | async-start | bytes 16777216 | tf_op jit(solution)/shard_map/all_to_all | solution.py:135
  31.1 0.0 copy-start.5
  31.1 0.0 copy-start
  31.1 0.0 copy-start.1
  31.1 0.0 all-reduce.3.cloned.1.call-start
  31.1 6.0 %copy.74 = bf16[512,3584]{1,0:T(8,128)(2,1)} copy(bf16[512,3584]{0,1:T(8,128)(2,1)} %bitcast.164) | data formatting | bytes 7340032 | tf_op jit(solution)/shard_map/reshape.100
  37.2 5.9 %copy.75 = bf16[512,3584]{1,0:T(8,128)(2,1)} copy(bf16[512,3584]{0,1:T(8,128)(2,1)} %bitcast.165) | data formatting | bytes 7340032 | tf_op jit(solution)/shard_map/reshape.113
  43.1 0.0 copy-done.5
  43.1 0.2 select_reduce_fusion
  43.3 0.0 copy-done
  43.3 0.2 fusion.14
  43.5 0.0 copy-done.1
  43.5 3.3 %convolution_bitcast_fusion.1 = f32[2,32,1,2,256]{4,1,3,0,2:T(8,128)S(1)} fusion(bf16[2,256,3584,1]{2,1,0,3:T(8,128)(2,1)} %bitcast.162, bf16[2,32,3584]{2,1,0:T(8,128)(2,1)S(1)} %copy-done, f32[3584]{0:T(1024)S(1)} %copy-done.1, f32[2,32]{1,0:T(2,128)S(1)} %add_rsqrt_fusion.2), kind=kOutput, calls=%fused_computation.13 | convolution fusion | flops 235798528 | bytes 4274432 | tf_op jit(solution)/shard_map/dot_general | solution.py:123
  46.8 0.2 fusion.50
  47.0 0.2 multiply_cosine_fusion.1
  47.2 3.3 %convolution_bitcast_fusion.2 = f32[2,32,1,2,256]{4,1,3,0,2:T(8,128)S(1)} fusion(bf16[2,256,3584,1]{2,1,0,3:T(8,128)(2,1)} %bitcast.161, bf16[2,32,3584]{2,1,0:T(8,128)(2,1)S(1)} %copy-done, f32[3584]{0:T(1024)S(1)} %copy-done.1, f32[2,32]{1,0:T(2,128)S(1)} %add_rsqrt_fusion.2), kind=kOutput, calls=%fused_computation.14 | convolution fusion | flops 235798528 | bytes 4274432 | tf_op jit(solution)/shard_map/dot_general | solution.py:120
  50.5 0.7 fusion.60
  51.3 0.1 copy.59
  51.4 0.1 fusion.30
  51.5 0.1 copy.65
  51.6 0.1 iota_compare_fusion.1
  51.7 80.5 %all-to-all-done = bf16[32,256,1,512]{3,1,2,0:T(8,128)(2,1)} async-done(((bf16[32,256,1,512]{3,1,2,0:T(8,128)(2,1)}), bf16[32,256,1,512]{3,1,2,0:T(8,128)(2,1)}, u32[]{:S(2)}, u32[]{:S(2)}) %all-to-all-start) | async-done | bytes 8388640 | tf_op jit(solution)/shard_map/all_to_all | solution.py:135
  132.2 8.4 %gather_fusion.1 = bf16[32,256,512]{2,1,0:T(8,128)(2,1)} fusion(bf16[32,256,512]{2,1,0:T(8,128)(2,1)} %bitcast.3, s32[1024]{0:T(1024)S(1)} %pad_clamp_fusion), kind=kCustom, calls=%fused_computation.1.clone | custom fusion | bytes 16777344 | tf_op jit(solution)/shard_map/jit(_take)/gather | solution.py:136
  140.6 7.5 %bitcast_select_fusion = bf16[32,256,1,512]{3,1,0,2:T(8,128)(2,1)} fusion(bf16[32,256,512]{2,1,0:T(8,128)(2,1)} %gather_fusion.1, pred[32]{0:T(512)(128)(4,1)S(1)} %get-tuple-element.5), kind=kLoop, calls=%fused_computation.2 | loop fusion | flops 4194304 | bytes 16777248 | tf_op jit(solution)/shard_map/jit(_take)/select_n | solution.py:136
  148.1 3.5 %fusion.59 = (f32[32,2,2]{2,1,0:T(2,128)S(1)}, f32[32,2,1,2,256]{4,3,1,0,2:T(2,128)S(1)}) fusion(bf16[2,32,2,256]{3,1,2,0:T(8,128)(2,1)S(1)} %pad_maximum_fusion, bf16[32,256,1,512]{3,1,0,2:T(8,128)(2,1)} %bitcast_select_fusion, pred[32,256]{1,0:T(8,128)(4,1)S(1)} %iota_compare_fusion.1), kind=kOutput, calls=%fused_computation.117 | convolution fusion | flops 16875392 | bytes 4399616 | tf_op jit(solution)/shard_map/vmap(tgrh,cgh->tgrc)/dot_general | solution.py:40
  151.6 0.1 copy.55
  151.7 0.3 fusion.21
  151.9 0.1 copy.64
  152.0 0.1 copy.60
  152.1 2.9 %fusion.7 = f32[2,32,1,2,256]{4,3,0,1,2:T(2,128)S(1)} fusion(bf16[32,256,1,512]{3,1,0,2:T(8,128)(2,1)} %bitcast_select_fusion, f32[32,2,1,2,256]{4,3,1,0,2:T(2,128)S(1)} %get-tuple-element.22, f32[32,2,2]{2,1,0:T(2,128)S(1)} %get-tuple-element.21, f32[2,32,2]{2,0,1:T(2,128)S(1)} %copy.60), kind=kOutput, calls=%fused_computation.19 | convolution fusion | flops 16875520 | bytes 4457472 | tf_op jit(solution)/shard_map/vmap(tgrc,cgh->tgrh)/dot_general | solution.py:48
  155.0 0.0 copy-start.2
  155.0 0.0 copy-start.3
  155.1 0.0 copy-start.4
  155.1 0.1 copy.66
  155.2 0.1 copy.61
  155.3 0.3 fusion.6
  155.7 2.8 %fusion.61 = f32[64,3584]{1,0:T(8,128)S(1)} fusion(bf16[64,512]{1,0:T(8,128)(2,1)S(1)} %bitcast.166, bf16[512,3584]{1,0:T(8,128)(2,1)} %param.20), kind=kOutput, calls=%fused_computation.119 | convolution fusion | flops 234881024 | bytes 4653056 | tf_op jit(solution)/shard_map/dot_general | solution.py:140
  158.5 1.0 slice_bitcast_fusion.16
  159.5 0.0 all-reduce.3.cloned.1.call-update
  159.5 78.2 %all-reduce.3.cloned.1.call-done = (f32[1,32,3584]{2,1,0:T(8,128)}, f32[1,32,3584]{2,1,0:T(8,128)}) async-done(((f32[1,32,3584]{2,1,0:T(8,128)}, f32[1,32,3584]{2,1,0:T(8,128)}), (f32[1,32,3584]{2,1,0:T(8,128)}, f32[1,32,3584]{2,1,0:T(8,128)})) %all-reduce.3.cloned.1.call-update) | async-done | bytes 917520 | tf_op jit(solution)/shard_map/psum | solution.py:143
  237.7 1.0 constant_dynamic-update-slice_fusion.1
  238.7 1.1 constant_dynamic-update-slice_fusion
  239.8 0.1 multiply_reduce_fusion.2
  239.9 0.0 copy-done.2
  239.9 0.3 multiply_reduce_fusion.1
  240.3 0.0 copy-done.3
  240.3 0.0 copy-done.4
  240.3 1.7 multiply_reduce_fusion
  (19 shorter events, 0.2 us)
Async XLA Ops:
  23.7 108.5 %all-to-all-start = ((bf16[32,256,1,512]{3,1,2,0:T(8,128)(2,1)}), bf16[32,256,1,512]{3,1,2,0:T(8,128)(2,1)}, u32[]{:S(2)}, u32[]{:S(2)}) async-start(bf16[32,256,1,512]{3,1,2,0:T(8,128)(2,1)} %bitcast_select_fusion.1), calls=%async_computation | async-start | bytes 16777216 | tf_op jit(solution)/shard_map/all_to_all | solution.py:135
  31.1 12.0 %copy-start.5 = (s32[1024]{0:T(1024)S(1)}, s32[1024]{0:T(1024)}, u32[]{:S(2)}) copy-start(s32[1024]{0:T(1024)} %param.15) | copy-start | bytes 12292
  31.1 12.2 %copy-start = (bf16[2,32,3584]{2,1,0:T(8,128)(2,1)S(1)}, bf16[2,32,3584]{2,1,0:T(8,128)(2,1)}, u32[]{:S(2)}) copy-start(bf16[2,32,3584]{2,1,0:T(8,128)(2,1)} %param.13) | copy-start | bytes 1376260
  31.1 12.4 %copy-start.1 = (f32[3584]{0:T(1024)S(1)}, f32[3584]{0:T(1024)}, u32[]{:S(2)}) copy-start(f32[3584]{0:T(1024)} %param.17) | copy-start | bytes 43012
  31.1 206.6 %all-reduce.3.cloned.1.call-start = ((), (), s32[]{:S(2)}) async-start(), calls=%async_computation.1 | async-start | bytes 1835008 | tf_op jit(solution)/shard_map/psum | solution.py:143
  155.0 84.9 %copy-start.2 = (f32[3584]{0:T(1024)S(1)}, f32[3584]{0:T(1024)}, u32[]{:S(2)}) copy-start(f32[3584]{0:T(1024)} %param.21) | copy-start | bytes 43012
  155.0 85.2 %copy-start.3 = (f32[3584]{0:T(1024)S(1)}, f32[3584]{0:T(1024)}, u32[]{:S(2)}) copy-start(f32[3584]{0:T(1024)} %param.23) | copy-start | bytes 43012
  155.1 85.2 %copy-start.4 = (f32[3584]{0:T(1024)S(1)}, f32[3584]{0:T(1024)}, u32[]{:S(2)}) copy-start(f32[3584]{0:T(1024)} %param.22) | copy-start | bytes 43012
Sparse Core Ops, SparseCore 0:
  159.6 77.9 all-reduce.2
where the time goes:
time: 250 us; the launch traced here: 249 us
  waiting for transfers between devices  159 us (64%)
  local copies, waits for them, and re-layouts  33.1 us (13%)
  other arithmetic  18.6 us (7%)
  matrix products  16.7 us (7%)
  between operations  14.3 us (6%)
  starting transfers between devices  7.37 us (3%)
    all_to_all x1, waiting for transfers between devices, per_device(): lax.all_to_all(served, 'dom', split_axis=0, concat_axis=0, tiled=True)  80.5 us
    psum x1, waiting for transfers between devices, per_device(): lax.psum(partial_proj[step], 'head')  78.2 us
    another operation x2, local copies, waits for them, and re-layouts  11.9 us
    gather x1, local copies, waits for them, and re-layouts, per_device(): blocks = jnp.take(received, source_dev, axis=0)  8.38 us
    gather x1, local copies, waits for them, and re-layouts, per_device(): served = jnp.take(kv_cache, chosen, axis=0)  8.17 us
    select_n x1, other arithmetic, per_device(): served = jnp.take(kv_cache, chosen, axis=0)  7.46 us
    select_n x1, other arithmetic, per_device(): blocks = jnp.take(received, source_dev, axis=0)  7.46 us
    all_to_all x1, starting transfers between devices, per_device(): lax.all_to_all(served, 'dom', split_axis=0, concat_axis=0, tiled=True)  7.33 us
  transfers between devices with their start and end apart: 2, of which 2 were waited for; matrix products, arithmetic and copies ran while one was open for 8% of the time, Pallas kernels for 0%

commit v1 on v0

v1 whole, which is shorter than its diff:
```python
import functools
import math

import jax
import jax.numpy as jnp
from jax import lax
from jax.experimental import pallas as pl
from jax.experimental.pallas import tpu as pltpu
from jax.sharding import PartitionSpec as P

EPSILON = 1e-06
SCORE_SCALE = 0.0625
MASKED_SCORE = -1e30
LOG_THETA = math.log(10000.0)
MESH = pl.DeviceIdType.MESH
F32 = jnp.float32
BF16 = jnp.bfloat16
CHUNKS = 7
WINDOW = 5


def iota(shape, dim):
    return lax.broadcasted_iota(jnp.int32, shape, dim)


def dot(a, b):
    return jnp.dot(a, b, preferred_element_type=F32)


def dot_t(a, b):
    return lax.dot_general(a, b, (((1,), (1,)), ((), ())), preferred_element_type=F32)


def split3(x):
    high = x.astype(BF16).astype(F32)
    rest = x - high
    mid = rest.astype(BF16).astype(F32)
    return (high, mid, rest - mid)


def kernel(
    grid3, anc_h, len_h, table_h, emb_h, gain_h, post_h, final_h, twist_h,
    wq_h, wkv_h, wo_h, kv_h, g_recv,
    anc_s, len_s, anc_v, gains, emb_b, x32, nrm, wq, wkv, wo, kv, a_v, a_s, q_send, q_recv, r_send, r_recv,
    rs_send, rs_mid, rs_half, rs_sum, rs_recv, g_send, g_mid,
    index_sem, gain_sem, emb_sem, w_sem, wo_sem, kv_sem, a_sem, q_ssem, q_rsem, r_ssem, r_rsem,
    rs_ssem, rs_rsem, g_ssem, g_rsem, own_sem,
):
    ny, nx, nc = grid3
    peers = ny * nx * nc
    local = peers
    heads = rs_send.shape[0]
    rows, width = emb_b.shape
    half = width // 2
    hd = kv.shape[2] // 2
    ctx = kv.shape[1]
    me = lax.axis_index("dom")
    head = lax.axis_index("head")
    my_y, my_x, my_c = me // (nx * nc), (me // nc) % nx, me % nc

    def ahead(i):
        y = (my_y + i // (nx * nc)) % ny
        x = (my_x + (i // nc) % nx) % nx
        return (y * nx + x) * nc + (my_c + i % nc) % nc

    def behind(i):
        y = (my_y + ny - i // (nx * nc)) % ny
        x = (my_x + nx - (i // nc) % nx) % nx
        return (y * nx + x) * nc + (my_c + nc - i % nc) % nc

    index_copies = [
        pltpu.make_async_copy(src, dst, index_sem.at[k])
        for k, (src, dst) in enumerate(((anc_h, anc_s), (len_h, len_s), (table_h, anc_v)))
    ]
    for copy in index_copies:
        copy.start()
    emb_copy = pltpu.make_async_copy(emb_h, emb_b, emb_sem)
    emb_copy.start()
    gain_copies = [
        pltpu.make_async_copy(src, gains.at[k, 0], gain_sem.at[k])
        for k, src in enumerate((gain_h, post_h, final_h, twist_h))
    ]
    for copy in gain_copies:
        copy.start()
    depth = width // CHUNKS
    w_copies = []
    for c in range(CHUNKS):
        part = pl.ds(c * depth, depth)
        pair = (
            pltpu.make_async_copy(wq_h.at[part], wq.at[part], w_sem.at[0, c]),
            pltpu.make_async_copy(wkv_h.at[part], wkv.at[part], w_sem.at[1, c]),
        )
        w_copies.append(pair)
    for pair in w_copies[:WINDOW]:
        for copy in pair:
            copy.start()
    kv_copy = pltpu.make_async_copy(kv_h, kv, kv_sem)
    wo_copy = pltpu.make_async_copy(wo_h, wo, wo_sem)

    barrier = pltpu.get_barrier_semaphore()

    def greet_dom(i, carry):
        pl.semaphore_signal(barrier, inc=1, device_id={"dom": ahead(i)}, device_id_type=MESH)
        return carry

    def greet_head(i, carry):
        pl.semaphore_signal(
            barrier, inc=1, device_id={"head": (head + i) % heads}, device_id_type=MESH
        )
        return carry

    lax.fori_loop(1, peers, greet_dom, 0)
    lax.fori_loop(1, heads, greet_head, 0)

    for copy in index_copies:
        copy.wait()
    table = anc_v[...]
    lines, lanes = table.shape
    lane = iota((lines, lanes), 1)
    hit = jnp.where(table // local == me, table % local, 0)
    picked = jnp.zeros((lines, lanes), jnp.int32)
    for q in range(lanes // local):
        best = jnp.max(jnp.where(lane // local == q, hit, 0), axis=1, keepdims=True)
        picked = jnp.where(lane == q, best, picked)
    a_v[...] = picked
    a_copy = pltpu.make_async_copy(a_v, a_s, a_sem)
    a_copy.start()

    sub = iota((local, 128), 0)
    lane = iota((local, 128), 1)
    source_col = jnp.zeros((local, 128), jnp.int32)
    source_row = jnp.zeros((local, 128), jnp.int32)
    length = jnp.zeros((local, 128), jnp.int32)
    for p in range(local):
        parent = anc_s[me * local + p]
        block = parent // local
        source_col = jnp.where(sub == p, block, source_col)
        source_row = jnp.where(lane % local == p, block, source_row)
        length = jnp.where(sub == p, len_s[parent], length)
    same = source_col == source_row
    rank_row = jnp.sum(jnp.where(same & (sub < lane % local), 1, 0), axis=0, keepdims=True)
    rank_col = jnp.sum(
        jnp.where(same & (lane < sub) & (lane < local), 1, 0), axis=1, keepdims=True
    )
    count = 4 * local
    turn = iota((1, count), 1) // local
    base_row = (source_row[0:1] * 8 + rank_row * 4)[:, :count]
    target_q = base_row + 2 * (turn % 2) + turn // 2
    target_n = source_row[0:1, :count] * 8 + 2 * rank_row[:, :count] + turn % 2 + 4 * (turn // 2)
    slot_row = iota((8 * peers, count), 0)
    gather_q = jnp.where(slot_row == target_q, 1.0, 0.0).astype(BF16)
    gather_n = jnp.where(slot_row == target_n, 1.0, 0.0).astype(BF16)
    base_col = source_col[:, 0:1] * 8 + rank_col * 4
    target_col = jnp.concatenate([base_col + (2 * t + r) for r in range(2) for t in range(2)], 0)
    scatter = jnp.where(iota((count, 8 * peers), 1) == target_col, 1.0, 0.0).astype(BF16)

    position = jnp.concatenate([length, length + 1], axis=0)[:, : hd // 2].astype(F32)
    inverse = jnp.exp(iota((1, hd // 2), 1).astype(F32) * (-LOG_THETA / (hd // 2)))
    angles = position * inverse
    cosine, sine = jnp.cos(angles), jnp.sin(angles)

    def rope(v):
        a, b = v[:, : hd // 2], v[:, hd // 2 :]
        return jnp.concatenate([a * cosine - b * sine, b * cosine + a * sine], axis=1)

    emb_copy.wait()
    for copy in gain_copies:
        copy.wait()
    attn_gain, post_gain, final_gain, twist_weight = (gains.at[k] for k in range(4))

    def norm_rows(i, carry):
        at = pl.ds(pl.multiple_of(i * 16, 16), 16)
        x = emb_b[at, :].astype(F32)
        x32[at, :] = x
        scale = lax.rsqrt(jnp.mean(x * x, axis=1, keepdims=True) + EPSILON)
        nrm[at, :] = (x * scale * attn_gain[...]).astype(BF16)
        return carry

    lax.fori_loop(0, rows // 16, norm_rows, 0)

    queries = jnp.zeros((rows, 2 * hd), F32)
    keyval = jnp.zeros((rows, 2 * hd), F32)
    for c in range(CHUNKS):
        part = slice(c * depth, (c + 1) * depth)
        for copy in w_copies[c]:
            copy.wait()
        if c + WINDOW < CHUNKS:
            for copy in w_copies[c + WINDOW]:
                copy.start()
        queries += dot(nrm[:, part], wq[part, :])
        keyval += dot(nrm[:, part], wkv[part, :])

    kv_copy.start()
    wo_copy.start()

    rotated = jnp.concatenate([rope(queries[:, :hd]), rope(queries[:, hd:])], axis=0)
    fresh = jnp.concatenate([rope(keyval[:, :hd]), keyval[:, hd:]], axis=0)
    q_send[:, :8] = dot(gather_q, rotated.astype(BF16)).reshape(peers, 8, hd).astype(BF16)
    q_send[:, 8:] = dot(gather_n, fresh.astype(BF16)).reshape(peers, 8, hd).astype(BF16)

    def q_copy(i, src, dst, dev):
        return pltpu.make_async_remote_copy(
            src_ref=q_send.at[src], dst_ref=q_recv.at[dst], send_sem=q_ssem.at[i],
            recv_sem=q_rsem.at[dst], device_id={"dom": dev}, device_id_type=MESH,
        )

    pl.semaphore_wait(barrier, peers + heads - 2)

    def q_start(i, carry):
        to = ahead(i)
        q_copy(to, to, me, to).start()
        return carry

    lax.fori_loop(1, peers, q_start, 0)
    q_recv[me] = q_send[me]

    a_copy.wait()
    kv_copy.wait()

    def r_copy(i, src, dst, dev):
        return pltpu.make_async_remote_copy(
            src_ref=r_send.at[src], dst_ref=r_recv.at[dst], send_sem=r_ssem.at[i],
            recv_sem=r_rsem.at[dst], device_id={"dom": dev}, device_id_type=MESH,
        )

    per_line = lanes // local
    lane8 = iota((8, ctx), 1)
    row, col = iota((128, 128), 0), iota((128, 128), 1)
    new = col % 16 - 8
    allowed = (row // 16 == col // 16) & (new >= 0) & (new < 4)
    allowed &= ((row % 8) // 4 == new // 2) & (new % 2 <= (row % 4) // 2)

    def attend(group, carry):
        def q_wait(slot, c):
            @pl.when(slot != me)
            def _():
                q_copy(slot, me, slot, slot).wait_recv()

            return c

        lax.fori_loop(group * 8, group * 8 + 8, q_wait, 0)
        slots, parents, scores, messages = [], [], [], []
        for j in range(8):
            slot = group * 8 + j
            parent = a_s[slot // per_line, slot % per_line]
            message = q_recv[slot]
            score = dot_t(message, kv[parent, :, :hd])[:8] * SCORE_SCALE
            scores.append(jnp.where(lane8 < len_s[me * local + parent], score, MASKED_SCORE))
            slots.append(slot)
            parents.append(parent)
            messages.append(message)
        score = jnp.concatenate(scores, axis=0)
        high_c = jnp.max(score, axis=1, keepdims=True)
        expo = jnp.exp(score - high_c)
        total_c = jnp.sum(expo, axis=1, keepdims=True)
        message = jnp.concatenate(messages, axis=0)
        fresh = jnp.where(allowed, dot_t(message, message) * SCORE_SCALE, MASKED_SCORE)
        high_n = jnp.max(fresh, axis=1, keepdims=True)
        expo_n = jnp.exp(fresh - high_n)
        total_n = jnp.sum(expo_n, axis=1, keepdims=True)
        out_n = dot(pltpu.roll(expo_n, 4, 1).astype(BF16), message)

        def queries_of(v):
            return v.reshape(8, 16, v.shape[1])[:, :8].reshape(64, v.shape[1])

        high_n, total_n, out_n = queries_of(high_n), queries_of(total_n), queries_of(out_n)
        highest = jnp.maximum(high_c, high_n)
        factor_c = jnp.exp(high_c - highest)
        factor_n = jnp.exp(high_n - highest)
        total = factor_c * total_c + factor_n * total_n
        for j in range(8):
            at = slice(8 * j, 8 * j + 8)
            out = dot(expo[at].astype(BF16), kv[parents[j], :, hd:])
            out = (factor_c[at] * out + factor_n[at] * out_n[at]) / total[at]
            r_send[slots[j]] = jnp.concatenate(
                [out[:, : hd // 2], out[:, hd // 2 :]], axis=0
            ).astype(BF16)

        def r_start(slot, c):
            @pl.when(slot != me)
            def _():
                r_copy(slot, slot, me, slot).start()

            return c

        lax.fori_loop(group * 8, group * 8 + 8, r_start, 0)
        return carry

    lax.fori_loop(0, peers // 8, attend, 0)
    r_recv[me] = r_send[me]

    def r_wait(i, carry):
        r_copy(i, me, ahead(i), ahead(i)).wait_recv()
        return carry

    lax.fori_loop(1, peers, r_wait, 0)

    back = r_recv[...].astype(F32)
    back = jnp.concatenate(
        [back[:, :8].reshape(8 * peers, hd // 2), back[:, 8:].reshape(8 * peers, hd // 2)], axis=1
    ).astype(BF16)
    attended = dot(scatter, back)
    attended = jnp.concatenate([attended[:rows], attended[rows:]], axis=1).astype(BF16)

    wo_copy.wait()
    step = 256
    for c in range(0, half, step):
        low = dot(attended, wo[:, c : c + step]).reshape(heads, 8, step)
        upper = dot(attended, wo[:, half + c : half + c + step]).reshape(heads, 8, step)
        rs_send[:, :, c : c + step] = jnp.concatenate([low, upper], axis=1).astype(BF16)

    quarter = half // 2
    part = (pl.ds(0, quarter), pl.ds(quarter, half - quarter))

    def around(d):
        return (head + heads + d) % heads

    def to_head(k, src, dst, send_sem, recv_sem, d):
        return pltpu.make_async_remote_copy(
            src_ref=src, dst_ref=dst, send_sem=send_sem.at[k], recv_sem=recv_sem.at[k],
            device_id={"head": around(d)}, device_id_type=MESH,
        )

    def rs_copy(k, src, dst, d):
        return to_head(k, src, dst, rs_ssem, rs_rsem, d)

    ways = ((0, 1), (1, -1))
    plain = [
        rs_copy(k, rs_send.at[around(3 * d), :, part[1 - k]], rs_mid.at[k, :, part[1 - k]], d)
        for k, d in ways
    ]
    fourth = [rs_copy(2 + k, rs_send.at[around(4), :, part[k]], rs_half.at[k], 2 * d) for k, d in ways]
    third = [
        rs_copy(4 + k, rs_send.at[around(3 * d), :, part[k]], rs_mid.at[k, :, part[k]], d)
        for k, d in ways
    ]
    direct = [rs_copy(6 + k, rs_send.at[around(d)], rs_recv.at[k], d) for k, d in ways]
    for copy in plain + fourth + third + direct:
        copy.start()
    late = []

    def hand_on(n, k, d, at, more):
        block = rs_send[around(2 * d), :, at].astype(F32) + rs_mid[k, :, at].astype(F32)
        if more:
            block += rs_half[k].astype(F32)
        rs_sum[k, :, at] = block.astype(BF16)
        copy = rs_copy(n, rs_sum.at[k, :, at], rs_recv.at[2 + k, :, at], 2 * d)
        copy.start()
        late.append(copy)

    for k, d in ways:
        plain[k].wait_recv()
        hand_on(8 + k, k, d, part[1 - k], False)
    for k, d in ways:
        fourth[k].wait_recv()
        third[k].wait_recv()
        hand_on(10 + k, k, d, part[k], True)
    for copy in direct:
        copy.wait_recv()
    projected = rs_send[head].astype(F32) + rs_recv[0].astype(F32) + rs_recv[1].astype(F32)
    for copy in late:
        copy.wait_recv()
    projected += rs_recv[2].astype(F32) + rs_recv[3].astype(F32)

    low, upper = projected[:8], projected[8:]

    def row_scale(a, b):
        square = jnp.sum(a * a, axis=1, keepdims=True) + jnp.sum(b * b, axis=1, keepdims=True)
        return lax.rsqrt(square * (1.0 / width) + EPSILON)

    mine = pl.ds(pl.multiple_of(head * 8, 8), 8)
    scale = row_scale(low, upper)
    low = x32[mine, :half] + low * scale * post_gain[:, :half]
    upper = x32[mine, half:] + upper * scale * post_gain[:, half:]
    scale = row_scale(low, upper)
    twist = jnp.sum(
        low * scale * final_gain[:, :half] * twist_weight[:, :half], axis=1, keepdims=True
    ) + jnp.sum(
        upper * scale * final_gain[:, half:] * twist_weight[:, half:], axis=1, keepdims=True
    )
    lane = iota((8, 128), 1)
    coded = jnp.zeros((8, 128), F32)
    for k, value in enumerate(split3(twist)):
        coded = jnp.where(lane == k, value, coded)
    g_send[:, :half] = jnp.concatenate([low, upper], axis=0).astype(BF16)
    g_send[:, half:] = jnp.concatenate([coded, jnp.zeros((8, 128), F32)], axis=0).astype(BF16)

    def g_copy(k, src, dst, d):
        return to_head(k, src, dst, g_ssem, g_rsem, d)

    part = (pl.ds(0, quarter), pl.ds(quarter, half + 128 - quarter))
    first = [g_copy(k, g_send.at[:, part[k]], g_mid.at[k, :, part[k]], 2 * d) for k, d in ways]
    first += [
        g_copy(2 + k, g_send.at[:, part[1 - k]], g_mid.at[k, :, part[1 - k]], 2 * d)
        for k, d in ways
    ]
    first += [g_copy(4 + k, g_send, g_recv.at[head], d) for k, d in ways]
    for copy in first:
        copy.start()
    own = [pltpu.make_async_copy(g_send, g_recv.at[head], own_sem.at[4])]
    own[0].start()
    second = []
    for n in range(4):
        k, d = ways[n % 2]
        at = part[k] if n < 2 else part[1 - k]
        first[n].wait_recv()
        here, there = g_mid.at[k, :, at], g_recv.at[around(-2 * d), :, at]
        new = [g_copy(6 + k, here, there, 2 * d)] if n < 2 else []
        new.append(g_copy(8 + n, here, there, d))
        for copy in new:
            copy.start()
        second += new
        own.append(pltpu.make_async_copy(here, there, own_sem.at[n]))
        own[-1].start()
    for copy in first[4:] + second:
        copy.wait_recv()
    for copy in own:
        copy.wait()

    def finish_dom(i, carry):
        to = ahead(i)
        q_copy(to, me, me, to).wait_send()
        r_copy(to, me, me, to).wait_send()
        return carry

    lax.fori_loop(1, peers, finish_dom, 0)
    for copy in plain + fourth + third + direct + late + first + second:
        copy.wait_send()


def order_rows(g_ref, out_v, twist_v):
    heads, half = g_ref.shape[0], g_ref.shape[2] - 128
    steps, local = twist_v.shape
    rows = steps * local
    for j in range(0, heads, 2):
        pair = [g_ref[k, :, :half].astype(F32) for k in (j, j + 1)]
        at = slice(8 * j, 8 * j + 16)
        out_v[at, :half] = jnp.concatenate([v[:8] for v in pair], axis=0).astype(BF16)
        out_v[at, half:] = jnp.concatenate([v[8:] for v in pair], axis=0).astype(BF16)
    coded = jnp.concatenate([g_ref[k, :, half:].astype(F32)[:8] for k in range(heads)], axis=0)
    twist = coded[:, 0:1] + coded[:, 1:2] + coded[:, 2:3]
    spread = jnp.where(iota((rows, 128), 0) % local == iota((rows, 128), 1), twist, 0.0)
    twist_v[...] = jnp.sum(spread.reshape(steps, local, 128), axis=1)[:, :local]


def per_device(
    grid3, embeds, ancestors, lengths, kv_cache, attn_gain, w_query, w_keyval, w_out,
    post_gain, final_gain, twist_weight,
):
    steps, local, width = embeds.shape
    ctx, hd2 = kv_cache.shape[1], kv_cache.shape[3]
    peers = lax.axis_size("dom")
    heads = lax.axis_size("head")
    rows = steps * local
    half = width // 2
    lanes = min(128, ancestors.shape[0])
    lines = ancestors.shape[0] // lanes
    vmem = pl.BlockSpec(memory_space=pltpu.VMEM)
    hbm = pl.BlockSpec(memory_space=pltpu.HBM)
    dma = pltpu.SemaphoreType.DMA
    gathered = pl.pallas_call(
        functools.partial(kernel, grid3),
        out_shape=jax.ShapeDtypeStruct((heads, 16, half + 128), BF16),
        in_specs=[hbm, hbm, hbm, hbm, hbm, hbm, hbm, hbm, hbm, hbm, hbm, hbm],
        out_specs=hbm,
        scratch_shapes=[
            pltpu.SMEM(ancestors.shape, jnp.int32),
            pltpu.SMEM(lengths.shape, jnp.int32),
            pltpu.VMEM((lines, lanes), jnp.int32),
            pltpu.VMEM((4, 1, width), F32),
            pltpu.VMEM((rows, width), BF16),
            pltpu.VMEM((rows, width), F32),
            pltpu.VMEM((rows, width), BF16),
            pltpu.VMEM(w_query.shape, BF16),
            pltpu.VMEM(w_keyval.shape, BF16),
            pltpu.VMEM(w_out.shape, BF16),
            pltpu.VMEM((local, ctx, hd2), BF16),
            pltpu.VMEM((lines, lanes), jnp.int32),
            pltpu.SMEM((lines, lanes), jnp.int32),
            pltpu.VMEM((peers, 16, hd2 // 2), BF16),
            pltpu.VMEM((peers, 16, hd2 // 2), BF16),
            pltpu.VMEM((peers, 16, hd2 // 4), BF16),
            pltpu.VMEM((peers, 16, hd2 // 4), BF16),
            pltpu.VMEM((heads, 16, half), BF16),
            pltpu.VMEM((2, 16, half), BF16),
            pltpu.VMEM((2, 16, half // 2), BF16),
            pltpu.VMEM((2, 16, half), BF16),
            pltpu.VMEM((4, 16, half), BF16),
            pltpu.VMEM((16, half + 128), BF16),
            pltpu.VMEM((2, 16, half + 128), BF16),
            dma((3,)), dma((4,)), dma, dma((2, CHUNKS)), dma, dma, dma,
            dma((peers,)), dma((peers,)), dma((peers,)), dma((peers,)),
            dma((12,)), dma((12,)), dma((12,)), dma((12,)), dma((5,)),
        ],
        compiler_params=pltpu.CompilerParams(
            collective_id=0, has_side_effects=True, vmem_limit_bytes=56 * 1024 * 1024
        ),
    )(
        ancestors, lengths, ancestors.reshape(lines, lanes), embeds.reshape(rows, width),
        attn_gain, post_gain,
        final_gain, twist_weight,
        w_query, w_keyval, w_out, kv_cache.reshape(local, ctx, hd2),
    )
    hidden, twist = pl.pallas_call(
        order_rows,
        out_shape=(
            jax.ShapeDtypeStruct((rows, width), BF16),
            jax.ShapeDtypeStruct((steps, local), F32),
        ),
        in_specs=[vmem],
        out_specs=(vmem, vmem),
        compiler_params=pltpu.CompilerParams(vmem_limit_bytes=56 * 1024 * 1024),
    )(gathered)
    return (hidden.reshape(steps, local, width), twist)


def solution(mesh):
    side = math.isqrt(mesh.shape["dom"] // 2)
    grid3 = (mesh.shape["dom"] // (2 * side), side, 2)
    in_specs = (
        P(None, "dom", None), P(), P(), P("dom", None, "head", None), P(), P(None, "head"),
        P(None, "head"), P("head", None), P(), P(), P(),
    )
    out_specs = (P(None, "dom", None), P(None, "dom"))
    return jax.shard_map(
        functools.partial(per_device, grid3), mesh=mesh, in_specs=in_specs, out_specs=out_specs,
        check_vma=False,
    )
```

time: 250 us -> 47.9 us (0.19)
  waiting for transfers between devices: 159 us -> 0 us
  Pallas kernels: 0 us -> 47.1 us
  local copies, waits for them, and re-layouts: 33.1 us -> 0 us
  other arithmetic: 18.6 us -> 0 us
  matrix products: 16.7 us -> 0 us
  between operations: 14.3 us -> 0.64 us
  starting transfers between devices: 7.37 us -> 0 us
    all_to_all x1 -> x0, waiting for transfers between devices: 80.5 us -> none  [per_device(): lax.all_to_all(served, 'dom', split_axis=0, concat_axis=0, tiled=True)]
    psum x1 -> x0, waiting for transfers between devices: 78.2 us -> none  [per_device(): lax.psum(partial_proj[step], 'head')]
    pallas_call x0 -> x2, Pallas kernels: none -> 47.1 us  [the longest x1 45.2 us: per_device(): pl.pallas_call(functools.partial(kernel, grid3), out_shape=jax.ShapeDtype...]
    dot_general x7 -> x0, matrix products: 16.7 us -> none  [the longest x1 3.48 us: prefix_partial(): jnp.einsum('tgrh,cgh->tgrc', queries, cached_keys, preferred_element_type...]
    gather x2 -> x0, local copies, waits for them, and re-layouts: 16.6 us -> none  [the longest x1 8.38 us: per_device(): blocks = jnp.take(received, source_dev, axis=0)]
    select_n x2 -> x0, other arithmetic: 14.9 us -> none  [the longest x1 7.46 us: per_device(): served = jnp.take(kv_cache, chosen, axis=0)]
    another operation x4 -> x0, local copies, waits for them, and re-layouts: 14 us -> none
    all_to_all x1 -> x0, starting transfers between devices: 7.33 us -> none  [per_device(): lax.all_to_all(served, 'dom', split_axis=0, concat_axis=0, tiled=True)]
  transfers between devices with their start and end apart: 2 -> 0, of which waited for: 2 -> 0; matrix products, arithmetic and copies ran while one was open for 8% -> 0% of each run, Pallas kernels for 0% -> 0%
where the time goes in v1:
time: 47.9 us; the launch traced here: 47.7 us
  Pallas kernels  47.1 us (98%)
  between operations  0.64 us (1%)
    pallas_call x1, Pallas kernels, per_device(): pl.pallas_call(functools.partial(kernel, grid3), out_shape=jax.ShapeDtype...  45.2 us
    pallas_call x1, Pallas kernels, per_device(): pl.pallas_call(order_rows, out_shape=(jax.ShapeDtypeStruct((rows, width),...  1.88 us

profile of v1, /device:TPU:24, one launch (start us, length us, event | category | flops | bytes accessed | tf_op | source)
XLA Modules:
  0.0 47.7 jit_solution(11284131790919623016)
XLA Ops:
  0.6 45.2 %shard_map.122.g_ref = bf16[8,16,1920]{2,1,0:T(8,128)(2,1)} custom-call(s32[1024]{0:T(1024)} %anc_h.1, s32[1024]{0:T(1024)} %len_h.1, s32[8,128]{1,0:T(8,128)} %bitcast.6, bf16[64,3584]{1,0:T(8,128)(2,1)} %bitcast.5, f32[3584]{0:T(1024)} %gain_h.1, f32[3584]{0:T(1024)} %post_h.1, f32[3584]{0:T(1024)} %final_h.1, f32[3584]{0:T(1024)} %twist_h.1, ...), custom_call_target="tpu_custom_call" | custom-call | tf_op jit(solution)/shard_map/pallas_call | solution.py:461
  45.8 1.9 %shard_map.123 = (bf16[64,3584]{1,0:T(8,128)(2,1)}, f32[2,32]{1,0:T(2,128)}) custom-call(bf16[8,16,1920]{2,1,0:T(8,128)(2,1)} %shard_map.122.g_ref), custom_call_target="tpu_custom_call" | custom-call | tf_op jit(solution)/shard_map/pallas_call | solution.py:504

commit v2 on v1

--- a/solution.py
+++ b/solution.py
@@ -15,8 +15,7 @@
 MESH = pl.DeviceIdType.MESH
 F32 = jnp.float32
 BF16 = jnp.bfloat16
-CHUNKS = 7
-WINDOW = 5
+CHUNKS = 2
 
 
 def iota(shape, dim):
@@ -84,16 +83,13 @@
         copy.start()
     depth = width // CHUNKS
     w_copies = []
-    for c in range(CHUNKS):
-        part = pl.ds(c * depth, depth)
-        pair = (
-            pltpu.make_async_copy(wq_h.at[part], wq.at[part], w_sem.at[0, c]),
-            pltpu.make_async_copy(wkv_h.at[part], wkv.at[part], w_sem.at[1, c]),
+    for k, (src, dst) in enumerate(((wq_h, wq), (wkv_h, wkv))):
+        part = [pl.ds(c * depth, depth) for c in range(CHUNKS)]
+        w_copies.append(
+            [pltpu.make_async_copy(src.at[p], dst.at[p], w_sem.at[k, c]) for c, p in enumerate(part)]
         )
-        w_copies.append(pair)
-    for pair in w_copies[:WINDOW]:
-        for copy in pair:
-            copy.start()
+    for copy in w_copies[0]:
+        copy.start()
     kv_copy = pltpu.make_async_copy(kv_h, kv, kv_sem)
     wo_copy = pltpu.make_async_copy(wo_h, wo, wo_sem)
 
@@ -163,6 +159,8 @@
         a, b = v[:, : hd // 2], v[:, hd // 2 :]
         return jnp.concatenate([a * cosine - b * sine, b * cosine + a * sine], axis=1)
 
+    for copy in w_copies[1]:
+        copy.start()
     emb_copy.wait()
     for copy in gain_copies:
         copy.wait()
@@ -178,24 +176,20 @@
 
     lax.fori_loop(0, rows // 16, norm_rows, 0)
 
-    queries = jnp.zeros((rows, 2 * hd), F32)
-    keyval = jnp.zeros((rows, 2 * hd), F32)
-    for c in range(CHUNKS):
-        part = slice(c * depth, (c + 1) * depth)
-        for copy in w_copies[c]:
+    @pl.when(head < heads)
+    def _():
+        for copy in w_copies[0]:
             copy.wait()
-        if c + WINDOW < CHUNKS:
-            for copy in w_copies[c + WINDOW]:
-                copy.start()
-        queries += dot(nrm[:, part], wq[part, :])
-        keyval += dot(nrm[:, part], wkv[part, :])
-
+        queries = dot(nrm[...], wq[...])
+        rotated = jnp.concatenate([rope(queries[:, :hd]), rope(queries[:, hd:])], axis=0)
+        q_send[:, :8] = dot(gather_q, rotated.astype(BF16)).reshape(peers, 8, hd).astype(BF16)
+
+    for copy in w_copies[1]:
+        copy.wait()
     kv_copy.start()
     wo_copy.start()
-
-    rotated = jnp.concatenate([rope(queries[:, :hd]), rope(queries[:, hd:])], axis=0)
+    keyval = dot(nrm[...], wkv[...])
     fresh = jnp.concatenate([rope(keyval[:, :hd]), keyval[:, hd:]], axis=0)
-    q_send[:, :8] = dot(gather_q, rotated.astype(BF16)).reshape(peers, 8, hd).astype(BF16)
     q_send[:, 8:] = dot(gather_n, fresh.astype(BF16)).reshape(peers, 8, hd).astype(BF16)
 
     def q_copy(i, src, dst, dev):
@@ -304,12 +298,7 @@
 
     wo_copy.wait()
     step = 256
-    for c in range(0, half, step):
-        low = dot(attended, wo[:, c : c + step]).reshape(heads, 8, step)
-        upper = dot(attended, wo[:, half + c : half + c + step]).reshape(heads, 8, step)
-        rs_send[:, :, c : c + step] = jnp.concatenate([low, upper], axis=1).astype(BF16)
-
-    quarter = half // 2
+    quarter = (half // step + 1) // 2 * step
     part = (pl.ds(0, quarter), pl.ds(quarter, half - quarter))
 
     def around(d):
@@ -329,32 +318,45 @@
         rs_copy(k, rs_send.at[around(3 * d), :, part[1 - k]], rs_mid.at[k, :, part[1 - k]], d)
         for k, d in ways
     ]
-    fourth = [rs_copy(2 + k, rs_send.at[around(4), :, part[k]], rs_half.at[k], 2 * d) for k, d in ways]
+    fourth = [
+        rs_copy(2 + k, rs_send.at[around(4), :, part[k]], rs_half.at[k, :, part[k]], 2 * d)
+        for k, d in ways
+    ]
     third = [
         rs_copy(4 + k, rs_send.at[around(3 * d), :, part[k]], rs_mid.at[k, :, part[k]], d)
         for k, d in ways
     ]
     direct = [rs_copy(6 + k, rs_send.at[around(d)], rs_recv.at[k], d) for k, d in ways]
-    for copy in plain + fourth + third + direct:
+    for k in (1, 0):
+        for c in range(k * quarter, half if k else quarter, step):
+            low = dot(attended, wo[:, c : c + step]).reshape(heads, 8, step)
+            upper = dot(attended, wo[:, half + c : half + c + step]).reshape(heads, 8, step)
+            rs_send[:, :, c : c + step] = jnp.concatenate([low, upper], axis=1).astype(BF16)
+        for copy in (plain[1 - k], fourth[k], third[k]):
+            copy.start()
+    for copy in direct:
         copy.start()
     late = []
 
     def hand_on(n, k, d, at, more):
         block = rs_send[around(2 * d), :, at].astype(F32) + rs_mid[k, :, at].astype(F32)
         if more:
-            block += rs_half[k].astype(F32)
+            block += rs_half[k, :, at].astype(F32)
         rs_sum[k, :, at] = block.astype(BF16)
         copy = rs_copy(n, rs_sum.at[k, :, at], rs_recv.at[2 + k, :, at], 2 * d)
         copy.start()
         late.append(copy)
 
-    for k, d in ways:
-        plain[k].wait_recv()
-        hand_on(8 + k, k, d, part[1 - k], False)
-    for k, d in ways:
-        fourth[k].wait_recv()
-        third[k].wait_recv()
-        hand_on(10 + k, k, d, part[k], True)
+    plain[0].wait_recv()
+    hand_on(8, 0, 1, part[1], False)
+    fourth[1].wait_recv()
+    third[1].wait_recv()
+    hand_on(11, 1, -1, part[1], True)
+    plain[1].wait_recv()
+    hand_on(9, 1, -1, part[0], False)
+    fourth[0].wait_recv()
+    third[0].wait_recv()
+    hand_on(10, 0, 1, part[0], True)
     for copy in direct:
         copy.wait_recv()
     projected = rs_send[head].astype(F32) + rs_recv[0].astype(F32) + rs_recv[1].astype(F32)
@@ -483,7 +485,7 @@
             pltpu.VMEM((peers, 16, hd2 // 4), BF16),
             pltpu.VMEM((heads, 16, half), BF16),
             pltpu.VMEM((2, 16, half), BF16),
-            pltpu.VMEM((2, 16, half // 2), BF16),
+            pltpu.VMEM((2, 16, half), BF16),
             pltpu.VMEM((2, 16, half), BF16),
             pltpu.VMEM((4, 16, half), BF16),
             pltpu.VMEM((16, half + 128), BF16),

time: 47.9 us -> 47.6 us (level)
  no operation moved by 1% of the time
where the time goes in v2:
time: 47.6 us; the launch traced here: 47.5 us
  Pallas kernels  46.8 us (98%)
  between operations  0.64 us (1%)
    pallas_call x1, Pallas kernels, per_device(): pl.pallas_call(functools.partial(kernel, grid3), out_shape=jax.ShapeDtype...  44.9 us
    pallas_call x1, Pallas kernels, per_device(): pl.pallas_call(order_rows, out_shape=(jax.ShapeDtypeStruct((rows, width),...  1.88 us

profile of v2, /device:TPU:24, one launch (start us, length us, event | category | flops | bytes accessed | tf_op | source)
XLA Modules:
  0.0 47.5 jit_solution(6364773741793588383)
XLA Ops:
  0.6 44.9 %shard_map.122.g_ref = bf16[8,16,1920]{2,1,0:T(8,128)(2,1)} custom-call(s32[1024]{0:T(1024)} %anc_h.1, s32[1024]{0:T(1024)} %len_h.1, s32[8,128]{1,0:T(8,128)} %bitcast.6, bf16[64,3584]{1,0:T(8,128)(2,1)} %bitcast.5, f32[3584]{0:T(1024)} %gain_h.1, f32[3584]{0:T(1024)} %post_h.1, f32[3584]{0:T(1024)} %final_h.1, f32[3584]{0:T(1024)} %twist_h.1, ...), custom_call_target="tpu_custom_call" | custom-call | tf_op jit(solution)/shard_map/pallas_call | solution.py:463
  45.6 1.9 %shard_map.123 = (bf16[64,3584]{1,0:T(8,128)(2,1)}, f32[2,32]{1,0:T(2,128)}) custom-call(bf16[8,16,1920]{2,1,0:T(8,128)(2,1)} %shard_map.122.g_ref), custom_call_target="tpu_custom_call" | custom-call | tf_op jit(solution)/shard_map/pallas_call | solution.py:506

commit v3 on v2

--- a/solution.py
+++ b/solution.py
@@ -205,7 +205,12 @@
         q_copy(to, to, me, to).start()
         return carry
 
-    lax.fori_loop(1, peers, q_start, 0)
+    def hops(i):
+        y, x = i // (nx * nc), (i // nc) % nx
+        return min(y, ny - y) + min(x, nx - x)
+
+    for i in sorted(range(1, peers), key=lambda i: -hops(i)):
+        q_start(i, 0)
     q_recv[me] = q_send[me]
 
     a_copy.wait()
@@ -232,7 +237,8 @@
 
             return c
 
-        lax.fori_loop(group * 8, group * 8 + 8, q_wait, 0)
+        for j in range(8):
+            q_wait(group * 8 + j, 0)
         slots, parents, scores, messages = [], [], [], []
         for j in range(8):
             slot = group * 8 + j
@@ -277,7 +283,8 @@
 
             return c
 
-        lax.fori_loop(group * 8, group * 8 + 8, r_start, 0)
+        for j in range(8):
+            r_start(group * 8 + j, 0)
         return carry
 
     lax.fori_loop(0, peers // 8, attend, 0)

time: 47.6 us -> 47.1 us (0.989)
  Pallas kernels: 46.8 us -> 46.3 us
    pallas_call x1, Pallas kernels: 44.9 us -> 44.4 us  [per_device(): pl.pallas_call(functools.partial(kernel, grid3), out_shape=jax.ShapeDtype...]
where the time goes in v3:
time: 47.1 us; the launch traced here: 46.9 us
  Pallas kernels  46.3 us (98%)
  between operations  0.64 us (1%)
    pallas_call x1, Pallas kernels, per_device(): pl.pallas_call(functools.partial(kernel, grid3), out_shape=jax.ShapeDtype...  44.4 us
    pallas_call x1, Pallas kernels, per_device(): pl.pallas_call(order_rows, out_shape=(jax.ShapeDtypeStruct((rows, width),...  1.88 us

profile of v3, /device:TPU:24, one launch (start us, length us, event | category | flops | bytes accessed | tf_op | source)
XLA Modules:
  0.0 46.9 jit_solution(11282837511267227908)
XLA Ops:
  0.6 44.4 %shard_map.122.g_ref = bf16[8,16,1920]{2,1,0:T(8,128)(2,1)} custom-call(s32[1024]{0:T(1024)} %anc_h.1, s32[1024]{0:T(1024)} %len_h.1, s32[8,128]{1,0:T(8,128)} %bitcast.6, bf16[64,3584]{1,0:T(8,128)(2,1)} %bitcast.5, f32[3584]{0:T(1024)} %gain_h.1, f32[3584]{0:T(1024)} %post_h.1, f32[3584]{0:T(1024)} %final_h.1, f32[3584]{0:T(1024)} %twist_h.1, ...), custom_call_target="tpu_custom_call" | custom-call | tf_op jit(solution)/shard_map/pallas_call | solution.py:470
  45.1 1.9 %shard_map.123 = (bf16[64,3584]{1,0:T(8,128)(2,1)}, f32[2,32]{1,0:T(2,128)}) custom-call(bf16[8,16,1920]{2,1,0:T(8,128)(2,1)} %shard_map.122.g_ref), custom_call_target="tpu_custom_call" | custom-call | tf_op jit(solution)/shard_map/pallas_call | solution.py:513
